TPU v7x, 256 devices: a whole 4x4x8 slice. The times are simulated.
256 devices in a mesh: blk: 32 (over y, z), rep: 8 (over x, core).
Axes of the slice: x: 4, y: 4, z: 8, core: 2. Of those that a mesh axis runs over, the one named last changes fastest.
Arguments:
- node_feats: bfloat16 [65536, 128], P('blk'), may hold values from -6 to 6
- weight: bfloat16 [128, 256], replicated, may hold values from -0.5 to 0.5
- tile_values: bfloat16 [12288, 128, 128], P(('blk', 'rep')), may hold values from -0.109375 to 0.109375
- tile_rows: int32 [12288], P(('blk', 'rep')), may hold values from 0 to 15
- tile_cols: int32 [12288], P(('blk', 'rep')), may hold values from 0 to 511, as said below
- tile_count: int32 [256], P(('blk', 'rep')), may hold values from 12 to 48, as said below
- cotangent: bfloat16 [65536, 256], P('blk'), may hold values from -6 to 6
Outputs:
- layer_out: bfloat16 [65536, 256], P('blk')
- grad_weight: float32 [128, 256], replicated
- grad_feats: float32 [65536, 128], P(('blk', 'rep'))
Inputs may be any that keep to these rules, and one draw needn't show every extreme that they name: `tile_cols`: in each tile list at most 2 slots name tile columns of one node block; in every draw one node block is named by exactly 2 slots of every list. `tile_count`: some list is full in every draw.
All inputs are finite; a program needn't handle non-finite values.
Results may differ from a plain program's by a relative error of at most 0.006.
Values may be sent and summed in bfloat16 or wider, within the bound.
A program may use at most 64 MiB of HBM per device.

v0:
```python
import math

import jax
import jax.numpy as jnp
from jax import lax
from jax.sharding import PartitionSpec as P


def body(node_feats, weight, tile_values, tile_rows, tile_cols, tile_count, cotangent):
    rows_blk, fin = node_feats.shape
    tile = tile_values.shape[1]
    slots = tile_values.shape[0]
    blocks = lax.axis_size("blk")
    row_tiles = rows_blk // tile
    nodes = rows_blk * blocks
    most = max(2, (4 * slots + 3 * blocks - 1) // (3 * blocks))
    seats = blocks * most
    owner_of = tile_cols // row_tiles
    local_tile = tile_cols % row_tiles
    match = (owner_of[:, None] == jnp.arange(blocks, dtype=jnp.int32)[None, :]).astype(jnp.int32)
    before = jnp.cumsum(match, axis=0) - match
    rank = jnp.sum(before * match, axis=1)
    seat_of = owner_of * most + rank
    requests = jnp.zeros((seats,), jnp.int32).at[seat_of].set(local_tile).reshape(blocks, most)
    asked = lax.all_to_all(requests, "blk", split_axis=0, concat_axis=0, tiled=True).reshape(seats)
    gathered = lax.all_gather(node_feats, "blk", axis=0, tiled=True)
    source = gathered.reshape(nodes // tile, tile, fin)
    group = math.gcd(slots, 16)
    live_count = tile_count[0]
    turns = (live_count + group - 1) // group

    def pick(turn):
        start = turn * group
        values = lax.dynamic_slice_in_dim(tile_values, start, group, 0)
        row_ids = lax.dynamic_slice_in_dim(tile_rows, start, group, 0)
        wanted = lax.dynamic_slice_in_dim(tile_cols, start, group, 0)
        seat_ids = lax.dynamic_slice_in_dim(seat_of, start, group, 0)
        live = (start + jnp.arange(group, dtype=jnp.int32) < live_count).astype(jnp.float32)
        return (values, row_ids, wanted, seat_ids, live)

    def forward_step(turn, acc):
        values, row_ids, wanted, seat_ids, live = pick(turn)
        inputs = source[wanted]
        prod = jnp.einsum("kij,kjf->kif", values, inputs, preferred_element_type=jnp.float32)
        return acc.at[row_ids].add(prod * live[:, None, None])

    partial_agg = lax.fori_loop(
        0, turns, forward_step, jnp.zeros((row_tiles, tile, fin), jnp.float32)
    )
    summed = lax.psum(partial_agg.reshape(rows_blk, fin), "rep")
    aggregated = summed.astype(jnp.bfloat16)
    pre = jnp.dot(aggregated, weight, preferred_element_type=jnp.float32)
    layer_out = jax.nn.silu(pre).astype(jnp.bfloat16)
    sig = jax.nn.sigmoid(pre)
    dpre = (cotangent.astype(jnp.float32) * sig * (1.0 + pre * (1.0 - sig))).astype(jnp.bfloat16)
    scale = 1.0 / math.sqrt(nodes)
    share = rows_blk // lax.axis_size("rep")
    offset = lax.axis_index("rep") * share
    agg_part = lax.dynamic_slice_in_dim(aggregated, offset, share, 0)
    dpre_part = lax.dynamic_slice_in_dim(dpre, offset, share, 0)
    term = jnp.einsum("nf,nh->fh", agg_part, dpre_part, preferred_element_type=jnp.float32) * scale
    grad_weight = lax.psum(term, ("blk", "rep"))
    dagg = jnp.dot(dpre, weight.T, preferred_element_type=jnp.float32).astype(jnp.bfloat16)
    dagg_tiles = dagg.reshape(row_tiles, tile, fin)

    def backward_step(turn, acc):
        values, row_ids, wanted, seat_ids, live = pick(turn)
        pieces = dagg_tiles[row_ids]
        contrib = jnp.einsum("kji,kjf->kif", values, pieces, preferred_element_type=jnp.float32)
        return acc.at[seat_ids].add(contrib * live[:, None, None])

    outgoing = lax.fori_loop(0, turns, backward_step, jnp.zeros((seats, tile, fin), jnp.float32))
    returned = lax.all_to_all(
        outgoing.reshape(blocks, most, tile, fin), "blk", split_axis=0, concat_axis=0, tiled=True
    )
    owner_acc = (
        jnp.zeros((row_tiles, tile, fin), jnp.float32)
        .at[asked]
        .add(returned.reshape(seats, tile, fin))
    )
    grad_feats = lax.psum_scatter(
        owner_acc.reshape(rows_blk, fin), "rep", scatter_dimension=0, tiled=True
    )
    return (layer_out, grad_weight, grad_feats)


def solution(mesh):
    in_specs = (
        P("blk", None),
        P(),
        P(("blk", "rep"), None, None),
        P(("blk", "rep")),
        P(("blk", "rep")),
        P(("blk", "rep")),
        P("blk", None),
    )
    out_specs = (P("blk", None), P(), P(("blk", "rep"), None))
    return jax.shard_map(body, mesh=mesh, in_specs=in_specs, out_specs=out_specs, check_vma=False)
```

profile of v0, /device:TPU:1, one launch (start us, length us, event | category | flops | bytes accessed | tf_op | source)
XLA Modules:
  0.0 582.6 jit_solution(17842083249096996942)
XLA Ops:
  10.4 12.0 %all-to-all-start = ((s32[32,1,2]{2,1,0:T(1,128)}), s32[32,1,2]{2,1,0:T(1,128)S(1)}, u32[]{:S(2)}, u32[]{:S(2)}) async-start(s32[32,1,2]{2,1,0:T(1,128)} %bitcast.3), calls=%async_computation | async-start | bytes 32768 | tf_op jit(solution)/shard_map/all_to_all | solution.py:25
  23.1 131.6 %all-gather.2.cloned.1.call-done = bf16[65536,128]{1,0:T(8,128)(2,1)} async-done(((bf16[2048,128]{1,0:T(8,128)(2,1)}), bf16[65536,128]{1,0:T(8,128)(2,1)}) %all-gather.2.cloned.1.call-update) | async-done | bytes 16777232 | tf_op jit(solution)/shard_map/all_gather | solution.py:26
  154.8 32.5 %while.20 = (s32[]{:T(128)}, f32[16,128,128]{2,1,0:T(8,128)S(1)}, s32[]{:T(128)}, s32[48]{0:T(128)}, bf16[48,128,128]{2,1,0:T(8,128)(2,1)}, /*index=5*/s32[48]{0...) while((s32[]{:T(128)}, f32[16,128,128]{2,1,0:T(8,128)S(1)}, ...), condition=%wide.region_2.3_spmd, body=%wide.region_0.2_spmd.sunk | while | flops 67634328 | bytes 6296307 | solution.py:47
  154.8 0.8 compare_select_fusion.11
  155.5 6.4 %gather_fusion = bf16[16,128,128]{2,1,0:T(8,128)(2,1)S(1)} fusion(bf16[512,128,128]{2,1,0:T(8,128)(2,1)} %get-tuple-element.295, s32[1024]{0:T(1024)S(1)} %pad_clamp_fusion.4), kind=kCustom, calls=%fused_computation.clone.1 | custom fusion | bytes 1048640 | tf_op jit(solution)/shard_map/while/body/gather | solution.py:43
  162.6 1.3 convolution_multiply_fusion.5
  164.0 1.6 scatter_fusion
  165.6 0.8 compare_select_fusion.11
  166.4 6.4 %gather_fusion = bf16[16,128,128]{2,1,0:T(8,128)(2,1)S(1)} fusion(bf16[512,128,128]{2,1,0:T(8,128)(2,1)} %get-tuple-element.295, s32[1024]{0:T(1024)S(1)} %pad_clamp_fusion.4), kind=kCustom, calls=%fused_computation.clone.1 | custom fusion | bytes 1048640 | tf_op jit(solution)/shard_map/while/body/gather | solution.py:43
  173.5 1.3 convolution_multiply_fusion.5
  174.8 1.6 scatter_fusion
  177.2 6.4 %gather_fusion = bf16[16,128,128]{2,1,0:T(8,128)(2,1)S(1)} fusion(bf16[512,128,128]{2,1,0:T(8,128)(2,1)} %get-tuple-element.295, s32[1024]{0:T(1024)S(1)} %pad_clamp_fusion.4), kind=kCustom, calls=%fused_computation.clone.1 | custom fusion | bytes 1048640 | tf_op jit(solution)/shard_map/while/body/gather | solution.py:43
  184.3 1.3 convolution_multiply_fusion.5
  185.7 1.6 scatter_fusion
  187.3 50.1 %all-reduce.4 = bf16[2048,128]{1,0:T(8,128)(2,1)S(1)} all-reduce(f32[2048,128]{1,0:T(8,128)S(1)} %bitcast.21), channel_id=1, replica_groups=mesh['blk'=32,'rep'=8] {'rep'}, use_global_device_ids=true, to_apply=%region_3.4 | all-reduce | flops 262144 | bytes 1572864 | tf_op jit(solution)/shard_map/psum | solution.py:50
  237.4 3.6 multiply_convert_fusion
  241.4 2.5 broadcast_in_dim.24
  243.9 18.7 %while.21 = (s32[]{:T(128)}, f32[64,128,128]{2,1,0:T(8,128)}, s32[]{:T(128)}, s32[48]{0:T(128)S(1)}, bf16[48,128,128]{2,1,0:T(8,128)(2,1)}, /*index=5*/s32[48]{0...) while((s32[]{:T(128)}, f32[64,128,128]{2,1,0:T(8,128)}, ...), condition=%wide.region_10.11_spmd, body=%wide.region_8.10_spmd.sunk | while | flops 67634328 | bytes 6296307 | solution.py:72
  245.3 1.4 convolution_multiply_fusion.6
  246.7 3.4 scatter_fusion.1
  251.5 1.4 convolution_multiply_fusion.6
  252.9 3.4 scatter_fusion.1
  257.7 1.4 convolution_multiply_fusion.6
  259.1 3.4 scatter_fusion.1
  262.5 4.9 all-to-all-start.1
  268.8 1.7 convolution_multiply_fusion.2
  270.5 88.5 %all-to-all-done.1 = f32[32,2,128,128]{3,2,1,0:T(8,128)} async-done(((f32[32,2,128,128]{3,2,1,0:T(8,128)}), f32[32,2,128,128]{3,2,1,0:T(8,128)}, u32[]{:S(2)}, u32[]{:S(2)}) %all-to-all-start.1) | async-done | bytes 4194336 | tf_op jit(solution)/shard_map/all_to_all | solution.py:73
  359.2 8.8 %scatter_fusion.2 = f32[16,128,128]{2,1,0:T(8,128)S(1)} fusion(f32[16,128,128]{2,1,0:T(8,128)S(1)} %broadcast.77, s32[64]{0:T(128)S(1)} %fusion.7, f32[64,128,128]{2,1,0:T(8,128)} %bitcast.7), kind=kCustom, calls=%fused_computation.5 | custom fusion | flops 1048576 | bytes 12583168 | tf_op jit(solution)/shard_map/scatter-add | solution.py:79
  368.0 1.0 copy-done.1
  369.0 172.7 %all-reduce.3.cloned.1.call-done = f32[128,256]{1,0:T(8,128)} async-done(((f32[128,256]{1,0:T(8,128)}), f32[128,256]{1,0:T(8,128)}) %all-reduce.3.cloned.1.call-update) | async-done | bytes 131088 | tf_op jit(solution)/shard_map/psum | solution.py:62
  541.7 32.8 %reduce-scatter.2.cloned.1.call-done = f32[256,128]{1,0:T(8,128)} async-done(((f32[2048,128]{1,0:T(8,128)}), f32[256,128]{1,0:T(8,128)}) %reduce-scatter.2.cloned.1.call-update) | async-done | bytes 131088 | tf_op jit(solution)/shard_map/reduce_scatter | solution.py:81
  574.5 1.6 copy.34
  (47 shorter events, 12.1 us)
Async XLA Ops:
  7.2 230.2 %copy-start = (bf16[128,256]{1,0:T(8,128)(2,1)S(1)}, bf16[128,256]{1,0:T(8,128)(2,1)}, u32[]{:S(2)}) copy-start(bf16[128,256]{1,0:T(8,128)(2,1)} %param.12) | copy-start | bytes 196612
  7.2 147.5 %all-gather.2.cloned.1.call-start = ((), (), s32[]{:S(2)}) async-start(), calls=%async_computation.3 | async-start | bytes 17301504 | tf_op jit(solution)/shard_map/all_gather | solution.py:26
  10.4 252.2 %all-to-all-start = ((s32[32,1,2]{2,1,0:T(1,128)}), s32[32,1,2]{2,1,0:T(1,128)S(1)}, u32[]{:S(2)}, u32[]{:S(2)}) async-start(s32[32,1,2]{2,1,0:T(1,128)} %bitcast.3), calls=%async_computation | async-start | bytes 32768 | tf_op jit(solution)/shard_map/all_to_all | solution.py:25
  237.4 3.6 copy-start.2
  241.4 2.5 copy-start.3
  262.5 96.5 %all-to-all-start.1 = ((f32[32,2,128,128]{3,2,1,0:T(8,128)}), f32[32,2,128,128]{3,2,1,0:T(8,128)}, u32[]{:S(2)}, u32[]{:S(2)}) async-start(f32[32,2,128,128]{3,2,1,0:T(8,128)} %bitcast.22), calls=%async_computation.1 | async-start | bytes 8388608 | tf_op jit(solution)/shard_map/all_to_all | solution.py:73
  267.4 274.3 %all-reduce.3.cloned.1.call-start = ((), (), s32[]{:S(2)}) async-start(), calls=%async_computation.4 | async-start | bytes 262144 | tf_op jit(solution)/shard_map/psum | solution.py:62
  270.5 304.0 %reduce-scatter.2.cloned.1.call-start = ((), (), s32[]{:S(2)}) async-start(), calls=%async_computation.5 | async-start | bytes 1179648 | tf_op jit(solution)/shard_map/reduce_scatter | solution.py:81
  368.0 1.0 copy-start.1
Sparse Core Ops, SparseCore 0:
  10.6 144.0 all-gather.1
  274.3 267.3 all-reduce.2
  544.8 29.6 reduce-scatter.1
where the time goes:
time: 585 us; the launch traced here: 583 us
  waiting for transfers between devices  426 us (73%)
  blocking collectives  50.1 us (9%)
  other arithmetic  32 us (5%)
  local copies, waits for them, and re-layouts  28.5 us (5%)
  starting transfers between devices  17 us (3%)
  between operations  14.6 us (2%)
  matrix products  14 us (2%)
    psum x1, waiting for transfers between devices, body(): grad_weight = lax.psum(term, ('blk', 'rep'))  173 us
    all_gather x1, waiting for transfers between devices, body(): gathered = lax.all_gather(node_feats, 'blk', axis=0, tiled=True)  132 us
    all_to_all x1, waiting for transfers between devices, body(): lax.all_to_all(outgoing.reshape(blocks, most, tile, fin), 'blk', split_ax...  88.5 us
    psum x1, blocking collectives, body(): summed = lax.psum(partial_agg.reshape(rows_blk, fin), 'rep')  50.1 us
    reduce_scatter x1, waiting for transfers between devices, body(): lax.psum_scatter(owner_acc.reshape(rows_blk, fin), 'rep', scatter_dimensi...  32.8 us
    gather x3, local copies, waits for them, and re-layouts, forward_step(): inputs = source[wanted]  19.3 us
    all_to_all x1, starting transfers between devices, body(): lax.all_to_all(requests, 'blk', split_axis=0, concat_axis=0, tiled=True)  12 us
  transfers between devices with their start and end apart: 5, of which 4 were waited for; matrix products, arithmetic and copies ran while one was open for 12% of the time, Pallas kernels for 0%

commit v1 on v0

v1 whole, which is shorter than its diff:
```python
import functools
import math

import jax
import jax.numpy as jnp
from jax import lax
from jax.experimental import pallas as pl
from jax.experimental.pallas import tpu as pltpu
from jax.sharding import PartitionSpec as P

MESH = pl.DeviceIdType.MESH
BF = jnp.bfloat16
F32 = jnp.float32
NY, NZ, NX, NC = 4, 8, 4, 2
REP = NX * NC
ROWT = 16
T = 128
COPIES = 160
FWD = (0, 7, 1, 6, 2, 5, 3, 4)
BWD = (4, 3, 5, 2, 6, 1, 7, 0)


def kernel(
    feats, weight, values, meta, rq, cot,
    layer_out, grad_weight, grad_feats,
    fb0, fb1, fb2, fb3, fb4, fb5, fb6, fb7,
    sy, got, prod, acc, sb, rb, agg, dagg, gwa, gwy, gwz, gwr,
    bs, br, unp, blkp, sr, zs, zp, zm, xs, xr, half,
    send_sem, recv_sem, local_sem,
):
    blk = lax.axis_index("blk")
    rep = lax.axis_index("rep")
    y, z = blk // NZ, lax.rem(blk, NZ)
    x, c = rep // NC, lax.rem(rep, NC)
    fb = (fb0, fb1, fb2, fb3, fb4, fb5, fb6, fb7)
    used = []

    def at(yy, zz, xx, cc):
        return {"blk": yy * NZ + zz, "rep": xx * NC + cc}

    def ypeer(d):
        return at(lax.rem(y + d, NY), z, x, c)

    def zpeer(d):
        return at(y, lax.rem(z + d, NZ), x, c)

    def rpeer(d):
        return {"blk": blk, "rep": lax.rem(rep + d, REP)}

    sibling = at(y, z, x, 1 - c)

    def put(src, dst, device):
        n = len(used)
        copy = pltpu.make_async_remote_copy(
            src_ref=src, dst_ref=dst, send_sem=send_sem.at[n], recv_sem=recv_sem.at[n],
            device_id=device, device_id_type=MESH,
        )
        used.append(copy)
        copy.start()
        return copy

    own = pltpu.make_async_copy(feats, fb[0], local_sem.at[0])
    own.start()
    barrier = pltpu.get_barrier_semaphore()
    peers = (
        [ypeer(d) for d in range(1, NY)]
        + [zpeer(d) for d in range(1, NZ)]
        + [rpeer(d) for d in range(1, REP)]
    )
    for p in peers:
        pl.semaphore_signal(barrier, inc=1, device_id=p, device_id_type=MESH)
    pl.semaphore_wait(barrier, len(peers))

    own.wait()

    def chunk(j):
        return pl.ds(8 * c + 4 * j, 4)

    up, down = {}, {}
    for j in range(2):
        up[7, j] = put(fb[0].at[chunk(j)], fb[7].at[chunk(j)], zpeer(1))
        down[1, j] = put(fb[0].at[chunk(j)], fb[1].at[chunk(j)], zpeer(NZ - 1))
    shared = {}

    def arrive(e):
        for j in range(2):
            ring = up if e > 4 or (e == 4 and j == 0) else down
            ring[e, j].wait_recv()
            if e > 4 and (e > 5 or j == 0):
                up[e - 1, j] = put(fb[e].at[chunk(j)], fb[e - 1].at[chunk(j)], zpeer(1))
            if e < 4 and (e < 3 or j == 1):
                down[e + 1, j] = put(fb[e].at[chunk(j)], fb[e + 1].at[chunk(j)], zpeer(NZ - 1))
            shared[e, j] = put(fb[e].at[chunk(j)], fb[e].at[chunk(j)], sibling)

    def seat_of(d, e, k):
        return 2 * (lax.rem(y + d, NY) * NZ + lax.rem(z + e, NZ)) + k

    def ask_of(d, e, k):
        return rq[d, 2 * lax.rem(z + e, NZ) + k]

    sent = {}

    def pack(e):
        for d in range(1, NY):
            for k in range(2):
                sy[d - 1, e, k] = fb[e][ask_of(d, e, k)]
            sent[d, e] = put(sy.at[d - 1, e], got.at[NY - d, e], ypeer(d))
        for k in range(2):
            got[0, e, k] = fb[e][ask_of(0, e, k)]

    def spmm(e, first):
        for d in range(1, NY):
            sent[d, e].wait_recv()
        rows = []
        for d in range(NY):
            for k in range(2):
                seat = seat_of(d, e, k)
                prod[2 * d + k] = jnp.dot(
                    values[meta[0, seat]], got[d, e, k], preferred_element_type=F32
                )
                rows.append(meta[1, seat])

        def add(t, carry):
            total = jnp.zeros((T, T), F32) if first else acc[t]
            for i in range(2 * NY):
                total = total + prod[i] * jnp.where(rows[i] == t, 1.0, 0.0).astype(F32)
            acc[t] = total
            return carry

        lax.fori_loop(0, ROWT, add, 0)

    for i, e in enumerate(FWD):
        if e:
            arrive(e)
            if i >= 2:
                spmm(FWD[i - 2], i == 2)
            for j in range(2):
                shared[e, j].wait_recv()
        pack(e)
    spmm(FWD[-2], False)
    spmm(FWD[-1], False)

    def cast(t, carry):
        sb[t] = acc[t].astype(BF)
        return carry

    lax.fori_loop(0, ROWT, cast, 0)
    scattered = [
        put(sb.at[pl.ds(2 * lax.rem(rep + d, REP), 2)], rb.at[REP - d], rpeer(d))
        for d in range(1, REP)
    ]
    mine = acc[pl.ds(2 * rep, 2)]
    for d, copy in enumerate(scattered, 1):
        copy.wait_recv()
        mine = mine + rb[REP - d].astype(F32)
    agg[pl.ds(2 * rep, 2)] = mine.astype(BF)
    pair = agg.at[pl.ds(2 * rep, 2)]
    spread = [put(pair, pair, rpeer(d)) for d in range(1, REP)]
    for copy in spread:
        copy.wait_recv()

    gwa[...] = jnp.zeros_like(gwa)

    def dense(i, carry):
        rows = pl.ds(pl.multiple_of(i * 256, 256), 256)
        a = agg[pl.ds(2 * i, 2)].reshape(256, T)
        pre = jnp.dot(a, weight[...], preferred_element_type=F32)
        sig = jax.nn.sigmoid(pre)
        layer_out[rows, :] = (pre * sig).astype(BF)
        dpre = (cot[rows, :].astype(F32) * sig * (1.0 + pre * (1.0 - sig))).astype(BF)
        gwa[...] += lax.dot_general(a, dpre, (((0,), (0,)), ((), ())), preferred_element_type=F32)
        back = lax.dot_general(dpre, weight[...], (((1,), (1,)), ((), ())), preferred_element_type=F32)
        dagg[pl.ds(2 * i, 2)] = back.astype(BF).reshape(2, T, T)
        return carry

    lax.fori_loop(0, 8, dense, 0)

    strip = pl.ds(pl.multiple_of(16 * rep, 16), 16)
    gwy[pl.ds(y, 1)] = (gwa[strip, :] * (1.0 / 256.0))[None]
    gw_y = [put(gwy.at[pl.ds(y, 1)], gwy.at[pl.ds(y, 1)], ypeer(d)) for d in range(1, NY)]

    back_sent = {}

    def products(e):
        for d in (1, 2, 3, 0):
            for k in range(2):
                seat = seat_of(d, e, k)
                row = meta[1, seat]
                live = jnp.where(row < ROWT, 1.0, 0.0).astype(F32)
                out = lax.dot_general(
                    values[meta[0, seat]], dagg[lax.rem(row, ROWT)],
                    (((0,), (0,)), ((), ())), preferred_element_type=F32,
                )
                if d:
                    bs[d - 1, e, k] = (out * live).astype(BF)
                else:
                    br[0, e, k] = (out * live).astype(BF)
            if d:
                back_sent[d, e] = put(bs.at[d - 1, e], br.at[NY - d, e], ypeer(d))

    sib_sent = {}

    def place(t):
        return 8 * lax.rem(t // 2, 2) + 2 * (t // 4) + lax.rem(t, 2)

    def collect(e):
        ids = []
        for d in range(NY):
            if d:
                back_sent[NY - d, e].wait_recv()
            for k in range(2):
                unp[2 * d + k] = br[d, e, k].astype(F32)
                ids.append(place(ask_of(d, e, k)))

        def add(t, carry):
            total = jnp.zeros((T, T), F32)
            for i in range(2 * NY):
                total = total + unp[i] * jnp.where(ids[i] == t, 1.0, 0.0).astype(F32)
            blkp[e, t] = total.astype(BF)
            return carry

        lax.fori_loop(0, ROWT, add, 0)
        sib_sent[e] = put(blkp.at[e, pl.ds(8 * (1 - c), 8)], sr.at[e], sibling)

    zup, zdown = {}, {}

    def chain(e):
        sib_sent[e].wait_recv()
        if e == 0:
            for j in range(2):
                zup[0, j].wait_recv()
                zdown[0, j].wait_recv()

            def home(t, carry):
                half[t] = (
                    blkp[0, 8 * c + t].astype(F32) + sr[0, t].astype(F32)
                    + zp[0, t].astype(F32) + zm[0, t].astype(F32)
                )
                return carry

            lax.fori_loop(0, 8, home, 0)
            return
        for j in range(2):
            rising = e < 4 or (e == 4 and j == 0)
            begins = e == 4 or (e == 3 and j == 1) or (e == 5 and j == 0)
            if not begins:
                (zup if rising else zdown)[e, j].wait_recv()

            def step(t, carry):
                total = blkp[e, 8 * c + t].astype(F32) + sr[e, t].astype(F32)
                if not begins:
                    total = total + (zp if rising else zm)[e % 8, t].astype(F32)
                zs[e, t] = total.astype(BF)
                return carry

            lax.fori_loop(4 * j, 4 * j + 4, step, 0)
            piece = pl.ds(4 * j, 4)
            if rising:
                zup[e - 1, j] = put(zs.at[e, piece], zp.at[e - 1, piece], zpeer(1))
            else:
                zdown[(e + 1) % 8, j] = put(zs.at[e, piece], zm.at[(e + 1) % 8, piece], zpeer(NZ - 1))

    gw_z, gw_r = [], []

    def gw_second():
        for copy in gw_y:
            copy.wait_recv()
        gwz[pl.ds(z, 1)] = (gwy[0] + gwy[1] + gwy[2] + gwy[3])[None]
        for d in range(1, NZ):
            gw_z.append(put(gwz.at[pl.ds(z, 1)], gwz.at[pl.ds(z, 1)], zpeer(d)))

    def gw_third():
        for copy in gw_z:
            copy.wait_recv()
        total = gwz[0]
        for i in range(1, NZ):
            total = total + gwz[i]
        gwr[strip, :] = total
        for d in range(1, REP):
            gw_r.append(put(gwr.at[strip], gwr.at[strip], rpeer(d)))

    n = len(BWD)
    for i in range(n + 3):
        if i < n:
            products(BWD[i])
        if 2 <= i < n + 2:
            collect(BWD[i - 2])
        if 3 <= i:
            chain(BWD[i - 3])
        if i == 4:
            gw_second()
        if i == 7:
            gw_third()

    x_sent = []
    for d in range(1, NX):
        there = lax.rem(x + d, NX)
        xs[d - 1] = half[pl.ds(2 * there, 2)].astype(BF)
        x_sent.append(put(xs.at[d - 1], xr.at[NX - d], at(y, z, there, c)))
    total = half[pl.ds(2 * x, 2)]
    for copy in gw_r:
        copy.wait_recv()
    grad_weight[...] = gwr[...]
    for d, copy in enumerate(x_sent, 1):
        copy.wait_recv()
        total = total + xr[NX - d].astype(F32)
    grad_feats[...] = total.reshape(2 * T, T)
    for copy in used:
        copy.wait_send()


def body(node_feats, weight, tile_values, tile_rows, tile_cols, tile_count, cotangent):
    slots = tile_values.shape[0]
    slot = jnp.arange(slots, dtype=jnp.int32)
    live = slot < tile_count[0]
    owner = tile_cols // ROWT
    same = (owner[:, None] == owner[None, :]) & live[None, :] & (slot[None, :] < slot[:, None])
    rank = jnp.sum(same.astype(jnp.int32), axis=1)
    seat = jnp.where(live, 2 * owner + rank, -1)
    seats = 2 * NY * NZ
    hit = seat[None, :] == jnp.arange(seats, dtype=jnp.int32)[:, None]
    table = jnp.stack([slot, tile_rows - ROWT, tile_cols % ROWT])
    meta = jnp.sum(jnp.where(hit[None], table[:, None, :], 0), axis=2)
    meta = meta + jnp.array([0, ROWT, 0], jnp.int32)[:, None]
    asks = meta[2].reshape(NY, 2 * NZ)
    y = lax.axis_index("blk") // NZ
    asked = [lax.dynamic_slice_in_dim(asks, y, 1, 0)]
    for d in range(1, NY):
        row = lax.dynamic_slice_in_dim(asks, (y + NY - d) % NY, 1, 0)
        perm = [(b, (b - d * NZ) % (NY * NZ)) for b in range(NY * NZ)]
        asked.append(lax.ppermute(row, "blk", perm))
    rq = jnp.concatenate(asked, axis=0)

    vmem = pl.BlockSpec(memory_space=pltpu.VMEM)
    smem = pl.BlockSpec(memory_space=pltpu.SMEM)
    tiles = lambda *lead: pltpu.VMEM((*lead, T, T), BF)
    wide = lambda *lead: pltpu.VMEM((*lead, T, T), F32)
    outs = pl.pallas_call(
        kernel,
        out_shape=(
            jax.ShapeDtypeStruct((2048, 256), BF),
            jax.ShapeDtypeStruct((128, 256), F32),
            jax.ShapeDtypeStruct((256, 128), F32),
        ),
        in_specs=[vmem, vmem, vmem, smem, smem, vmem],
        out_specs=(vmem, vmem, vmem),
        scratch_shapes=[tiles(ROWT) for _ in range(8)] + [
            tiles(3, 8, 2), tiles(4, 8, 2), wide(8), wide(16),
            tiles(16), tiles(8, 2), tiles(16), tiles(16),
            pltpu.VMEM((128, 256), F32), pltpu.VMEM((NY, 16, 256), F32),
            pltpu.VMEM((NZ, 16, 256), F32), pltpu.VMEM((128, 256), F32),
            tiles(3, 8, 2), tiles(4, 8, 2), wide(8), tiles(8, 16), tiles(8, 8),
            tiles(8, 8), tiles(8, 8), tiles(8, 8), tiles(3, 2), tiles(4, 2), wide(8),
            pltpu.SemaphoreType.DMA((COPIES,)), pltpu.SemaphoreType.DMA((COPIES,)),
            pltpu.SemaphoreType.DMA((1,)),
        ],
        compiler_params=pltpu.CompilerParams(
            collective_id=1, has_side_effects=True, vmem_limit_bytes=56 << 20
        ),
        name="layer",
    )(node_feats.reshape(ROWT, T, T), weight, tile_values, meta[:2], rq, cotangent)
    return outs


def solution(mesh):
    in_specs = (
        P("blk", None),
        P(),
        P(("blk", "rep"), None, None),
        P(("blk", "rep")),
        P(("blk", "rep")),
        P(("blk", "rep")),
        P("blk", None),
    )
    out_specs = (P("blk", None), P(), P(("blk", "rep"), None))
    return jax.shard_map(body, mesh=mesh, in_specs=in_specs, out_specs=out_specs, check_vma=False)
```

time: 585 us -> 129 us (0.22)
  waiting for transfers between devices: 426 us -> 0.76 us
  Pallas kernels: 0 us -> 112 us
  blocking collectives: 50.1 us -> 0 us
  other arithmetic: 32 us -> 3.02 us
  local copies, waits for them, and re-layouts: 28.5 us -> 4.31 us
  matrix products: 14 us -> 0 us
  between operations: 14.6 us -> 1.41 us
  starting transfers between devices: 17 us -> 5.89 us
    psum x1 -> x0, waiting for transfers between devices: 173 us -> none  [body(): grad_weight = lax.psum(term, ('blk', 'rep'))]
    all_gather x1 -> x0, waiting for transfers between devices: 132 us -> none  [body(): gathered = lax.all_gather(node_feats, 'blk', axis=0, tiled=True)]
    pallas_call x0 -> x1, Pallas kernels: none -> 112 us  [body(): pl.pallas_call(kernel, out_shape=(jax.ShapeDtypeStruct((2048, 256), BF),...]
    all_to_all x2 -> x0, waiting for transfers between devices: 88.5 us -> none  [the longest x1 88.5 us: body(): lax.all_to_all(outgoing.reshape(blocks, most, tile, fin), 'blk', split_ax...]
    psum x1 -> x0, blocking collectives: 50.1 us -> none  [body(): summed = lax.psum(partial_agg.reshape(rows_blk, fin), 'rep')]
    reduce_scatter x1 -> x0, waiting for transfers between devices: 32.8 us -> none  [body(): lax.psum_scatter(owner_acc.reshape(rows_blk, fin), 'rep', scatter_dimensi...]
    scatter-add x7 -> x0, other arithmetic: 23.8 us -> none  [the longest x3 10.2 us: backward_step(): return acc.at[seat_ids].add(contrib * live[:, None, None])]
    gather x6 -> x0, local copies, waits for them, and re-layouts: 21.2 us -> none  [the longest x3 19.3 us: forward_step(): inputs = source[wanted]]
  transfers between devices with their start and end apart: 5 -> 3, of which waited for: 4 -> 1; matrix products, arithmetic and copies ran while one was open for 12% -> 0% of each run, Pallas kernels for 0% -> 0%
where the time goes in v1:
time: 129 us; the launch traced here: 127 us
  Pallas kernels  112 us (87%)
  starting transfers between devices  5.89 us (5%)
  local copies, waits for them, and re-layouts  4.31 us (3%)
  other arithmetic  3.02 us (2%)
  between operations  1.41 us (1%)
    pallas_call x1, Pallas kernels, body(): pl.pallas_call(kernel, out_shape=(jax.ShapeDtypeStruct((2048, 256), BF),...  112 us
    ppermute x3, starting transfers between devices, body(): asked.append(lax.ppermute(row, 'blk', perm))  5.89 us
    unnamed x7, local copies, waits for them, and re-layouts  3.62 us
  transfers between devices with their start and end apart: 3, of which 1 were waited for; matrix products, arithmetic and copies ran while one was open for 0% of the time, Pallas kernels for 0%

profile of v1, /device:TPU:1, one launch (start us, length us, event | category | flops | bytes accessed | tf_op | source)
XLA Modules:
  0.0 127.1 jit_solution(16614793491522144986)
XLA Ops:
  1.4 0.7 add_bitcast_fusion
  2.0 0.7 and_select_fusion.1
  2.7 0.2 convert_reduce_fusion
  2.9 0.1 iota_compare_fusion
  3.0 0.1 select_reduce_fusion
  3.1 0.7 broadcast_add_fusion
  3.8 0.1 reshape_squeeze.3
  3.9 2.2 %collective-permute-start.2 = (s32[1,16]{1,0:T(1,128)S(1)}, s32[1,16]{1,0:T(1,128)S(1)}, u32[]{:S(2)}, u32[]{:S(2)}) collective-permute-start(s32[1,16]{1,0:T(1,128)S(1)} %get-tuple-element.4), channel_id=1, source_target_pairs={{0,64},{8,72},{16,80},{24,88},{32,96},{40,104},{48,112},{56,120},{... | collective-permute-start | bytes 200 | tf_op jit(solution)/shard_map/ppermute | solution.py:331
  6.1 2.6 %collective-permute-start.1 = (s32[1,16]{1,0:T(1,128)S(1)}, s32[1,16]{1,0:T(1,128)S(1)}, u32[]{:S(2)}, u32[]{:S(2)}) collective-permute-start(s32[1,16]{1,0:T(1,128)S(1)} %get-tuple-element.5), channel_id=1, source_target_pairs={{0,128},{8,136},{16,144},{24,152},{32,160},{40,168},{48,176},{56,1... | collective-permute-start | bytes 200 | tf_op jit(solution)/shard_map/ppermute | solution.py:331
  8.8 1.1 collective-permute-start
  9.8 0.6 slice.6.meta
  10.4 0.0 collective-permute-done.2
  10.4 0.0 collective-permute-done.1
  10.4 0.8 collective-permute-done
  11.1 0.6 pad_add_fusion.1.rq
  11.7 111.7 %layer.1 = (bf16[2048,256]{1,0:T(8,128)(2,1)}, f32[128,256]{1,0:T(8,128)}, f32[256,128]{1,0:T(8,128)}) custom-call(bf16[16,128,128]{2,1,0:T(8,128)(2,1)} %bitcast.8, bf16[128,256]{1,0:T(8,128)(2,1)} %weight.1, bf16[48,128,128]{2,1,0:T(8,128)(2,1)} %values.1, s32[2,64]{1,0:T(2,128)} %slice.6.meta, s32[4,16]{1,0:T(4,128)} %pad_add_fusion.1.rq, ...), custom_call_target="tpu_custom_call" | custom-call | tf_op jit(solution)/shard_map/layer/pallas_call | solution.py:338
  123.4 0.0 copy-start.1
  123.5 0.0 copy-start
  123.5 2.3 %copy.15 = bf16[2048,256]{1,0:T(8,128)(2,1)} copy(bf16[2048,256]{1,0:T(8,128)(2,1)} %get-tuple-element.12) | data formatting | bytes 2097152
  125.8 0.0 copy-done.1
  125.8 0.7 copy.16
  126.4 0.0 copy-done
  126.4 0.7 copy.17
  (6 shorter events, 0.1 us)
Async XLA Ops:
  3.9 6.5 %collective-permute-start.2 = (s32[1,16]{1,0:T(1,128)S(1)}, s32[1,16]{1,0:T(1,128)S(1)}, u32[]{:S(2)}, u32[]{:S(2)}) collective-permute-start(s32[1,16]{1,0:T(1,128)S(1)} %get-tuple-element.4), channel_id=1, source_target_pairs={{0,64},{8,72},{16,80},{24,88},{32,96},{40,104},{48,112},{56,120},{... | collective-permute-start | bytes 200 | tf_op jit(solution)/shard_map/ppermute | solution.py:331
  6.1 4.3 %collective-permute-start.1 = (s32[1,16]{1,0:T(1,128)S(1)}, s32[1,16]{1,0:T(1,128)S(1)}, u32[]{:S(2)}, u32[]{:S(2)}) collective-permute-start(s32[1,16]{1,0:T(1,128)S(1)} %get-tuple-element.5), channel_id=1, source_target_pairs={{0,128},{8,136},{16,144},{24,152},{32,160},{40,168},{48,176},{56,1... | collective-permute-start | bytes 200 | tf_op jit(solution)/shard_map/ppermute | solution.py:331
  8.8 2.4 %collective-permute-start = (s32[1,16]{1,0:T(1,128)S(1)}, s32[1,16]{1,0:T(1,128)S(1)}, u32[]{:S(2)}, u32[]{:S(2)}) collective-permute-start(s32[1,16]{1,0:T(1,128)S(1)} %get-tuple-element.6), channel_id=1, source_target_pairs={{0,192},{8,200},{16,208},{24,216},{32,224},{40,232},{48,240},{56,2... | collective-permute-start | bytes 200 | tf_op jit(solution)/shard_map/ppermute | solution.py:331
  123.4 2.3 %copy-start.1 = (f32[128,256]{1,0:T(8,128)S(1)}, f32[128,256]{1,0:T(8,128)}, u32[]{:S(2)}) copy-start(f32[128,256]{1,0:T(8,128)} %get-tuple-element.13) | copy-start | bytes 393220
  123.5 3.0 %copy-start = (f32[256,128]{1,0:T(8,128)S(1)}, f32[256,128]{1,0:T(8,128)}, u32[]{:S(2)}) copy-start(f32[256,128]{1,0:T(8,128)} %get-tuple-element.14) | copy-start | bytes 393220

commit v2 on v1

--- a/solution.py
+++ b/solution.py
@@ -20,10 +20,40 @@
 BWD = (4, 3, 5, 2, 6, 1, 7, 0)
 
 
+def tables(tile_cols, tile_rows, count, metav, reqv, rqv):
+    n = tile_cols.shape[1]
+    across = lax.broadcasted_iota(jnp.int32, (n, n), 1)
+    along = lax.broadcasted_iota(jnp.int32, (n, n), 0)
+    live = count[0]
+
+    def column(row):
+        square = jnp.where(across == along, jnp.broadcast_to(row, (n, n)), 0)
+        return jnp.sum(square, axis=1, keepdims=True)
+
+    cols = tile_cols[...]
+    owner, within = cols >> 4, cols & 15
+    owner_c = column(owner)
+    same = (owner_c == jnp.broadcast_to(owner, (n, n))) & (across < along) & (across < live)
+    rank = jnp.sum(jnp.where(same, 1, 0), axis=1, keepdims=True)
+    slot = column(across[:1])
+    seat = jnp.where(slot < live, 2 * owner_c + rank, -1)
+    hit = seat == lax.broadcasted_iota(jnp.int32, (n, T), 1)
+
+    def spread(value):
+        return jnp.sum(jnp.where(hit, value, 0), axis=0, keepdims=True)
+
+    metav[pl.ds(0, 1), :] = spread(slot)
+    metav[pl.ds(1, 1), :] = spread(column(tile_rows[...]) - ROWT) + ROWT
+    asks = spread(column(within))
+    reqv[...] = asks
+    rqv[pl.ds(0, 1), :] = asks
+
+
 def kernel(
-    feats, weight, values, meta, rq, cot,
+    feats, weight, tile_values, tile_cols, tile_rows, count, cotangent,
     layer_out, grad_weight, grad_feats,
     fb0, fb1, fb2, fb3, fb4, fb5, fb6, fb7,
+    values, cot, lo, metav, meta, reqv, rqv, rq,
     sy, got, prod, acc, sb, rb, agg, dagg, gwa, gwy, gwz, gwr,
     bs, br, unp, blkp, sr, zs, zp, zm, xs, xr, half,
     send_sem, recv_sem, local_sem,
@@ -60,7 +90,11 @@
         return copy
 
     own = pltpu.make_async_copy(feats, fb[0], local_sem.at[0])
-    own.start()
+    load_values = pltpu.make_async_copy(tile_values, values, local_sem.at[1])
+    load_cot = pltpu.make_async_copy(cotangent, cot, local_sem.at[2])
+    load_meta = pltpu.make_async_copy(metav, meta, local_sem.at[3])
+    load_rq = pltpu.make_async_copy(rqv, rq, local_sem.at[4])
+    store_lo = pltpu.make_async_copy(lo, layer_out, local_sem.at[5])
     barrier = pltpu.get_barrier_semaphore()
     peers = (
         [ypeer(d) for d in range(1, NY)]
@@ -69,7 +103,14 @@
     )
     for p in peers:
         pl.semaphore_signal(barrier, inc=1, device_id=p, device_id_type=MESH)
+    own.start()
+    load_values.start()
+    load_cot.start()
+    tables(tile_cols, tile_rows, count, metav, reqv, rqv)
+    load_meta.start()
     pl.semaphore_wait(barrier, len(peers))
+
+    asked = [put(reqv, rqv.at[pl.ds(NY - d, 1)], ypeer(d)) for d in range(1, NY)]
 
     own.wait()
 
@@ -96,7 +137,10 @@
         return 2 * (lax.rem(y + d, NY) * NZ + lax.rem(z + e, NZ)) + k
 
     def ask_of(d, e, k):
-        return rq[d, 2 * lax.rem(z + e, NZ) + k]
+        return rq[d, seat_of(0, e, k)] & (ROWT - 1)
+
+    def slot_in(seat):
+        return jnp.clip(meta[0, seat], 0, values.shape[0] - 1)
 
     sent = {}
 
@@ -116,7 +160,7 @@
             for k in range(2):
                 seat = seat_of(d, e, k)
                 prod[2 * d + k] = jnp.dot(
-                    values[meta[0, seat]], got[d, e, k], preferred_element_type=F32
+                    values[slot_in(seat)], got[d, e, k], preferred_element_type=F32
                 )
                 rows.append(meta[1, seat])
 
@@ -136,6 +180,13 @@
                 spmm(FWD[i - 2], i == 2)
             for j in range(2):
                 shared[e, j].wait_recv()
+        else:
+            for copy in asked:
+                copy.wait_recv()
+            load_rq.start()
+            load_meta.wait()
+            load_values.wait()
+            load_rq.wait()
         pack(e)
     spmm(FWD[-2], False)
     spmm(FWD[-1], False)
@@ -160,13 +211,14 @@
         copy.wait_recv()
 
     gwa[...] = jnp.zeros_like(gwa)
+    load_cot.wait()
 
     def dense(i, carry):
         rows = pl.ds(pl.multiple_of(i * 256, 256), 256)
         a = agg[pl.ds(2 * i, 2)].reshape(256, T)
         pre = jnp.dot(a, weight[...], preferred_element_type=F32)
         sig = jax.nn.sigmoid(pre)
-        layer_out[rows, :] = (pre * sig).astype(BF)
+        lo[rows, :] = (pre * sig).astype(BF)
         dpre = (cot[rows, :].astype(F32) * sig * (1.0 + pre * (1.0 - sig))).astype(BF)
         gwa[...] += lax.dot_general(a, dpre, (((0,), (0,)), ((), ())), preferred_element_type=F32)
         back = lax.dot_general(dpre, weight[...], (((1,), (1,)), ((), ())), preferred_element_type=F32)
@@ -174,6 +226,7 @@
         return carry
 
     lax.fori_loop(0, 8, dense, 0)
+    store_lo.start()
 
     strip = pl.ds(pl.multiple_of(16 * rep, 16), 16)
     gwy[pl.ds(y, 1)] = (gwa[strip, :] * (1.0 / 256.0))[None]
@@ -188,7 +241,7 @@
                 row = meta[1, seat]
                 live = jnp.where(row < ROWT, 1.0, 0.0).astype(F32)
                 out = lax.dot_general(
-                    values[meta[0, seat]], dagg[lax.rem(row, ROWT)],
+                    values[slot_in(seat)], dagg[row & (ROWT - 1)],
                     (((0,), (0,)), ((), ())), preferred_element_type=F32,
                 )
                 if d:
@@ -305,34 +358,17 @@
         copy.wait_recv()
         total = total + xr[NX - d].astype(F32)
     grad_feats[...] = total.reshape(2 * T, T)
+    store_lo.wait()
     for copy in used:
         copy.wait_send()
 
 
 def body(node_feats, weight, tile_values, tile_rows, tile_cols, tile_count, cotangent):
     slots = tile_values.shape[0]
-    slot = jnp.arange(slots, dtype=jnp.int32)
-    live = slot < tile_count[0]
-    owner = tile_cols // ROWT
-    same = (owner[:, None] == owner[None, :]) & live[None, :] & (slot[None, :] < slot[:, None])
-    rank = jnp.sum(same.astype(jnp.int32), axis=1)
-    seat = jnp.where(live, 2 * owner + rank, -1)
-    seats = 2 * NY * NZ
-    hit = seat[None, :] == jnp.arange(seats, dtype=jnp.int32)[:, None]
-    table = jnp.stack([slot, tile_rows - ROWT, tile_cols % ROWT])
-    meta = jnp.sum(jnp.where(hit[None], table[:, None, :], 0), axis=2)
-    meta = meta + jnp.array([0, ROWT, 0], jnp.int32)[:, None]
-    asks = meta[2].reshape(NY, 2 * NZ)
-    y = lax.axis_index("blk") // NZ
-    asked = [lax.dynamic_slice_in_dim(asks, y, 1, 0)]
-    for d in range(1, NY):
-        row = lax.dynamic_slice_in_dim(asks, (y + NY - d) % NY, 1, 0)
-        perm = [(b, (b - d * NZ) % (NY * NZ)) for b in range(NY * NZ)]
-        asked.append(lax.ppermute(row, "blk", perm))
-    rq = jnp.concatenate(asked, axis=0)
-
     vmem = pl.BlockSpec(memory_space=pltpu.VMEM)
     smem = pl.BlockSpec(memory_space=pltpu.SMEM)
+    hbm = pl.BlockSpec(memory_space=pl.ANY)
+    ints = lambda space, n: space((n, T), jnp.int32)
     tiles = lambda *lead: pltpu.VMEM((*lead, T, T), BF)
     wide = lambda *lead: pltpu.VMEM((*lead, T, T), F32)
     outs = pl.pallas_call(
@@ -342,9 +378,12 @@
             jax.ShapeDtypeStruct((128, 256), F32),
             jax.ShapeDtypeStruct((256, 128), F32),
         ),
-        in_specs=[vmem, vmem, vmem, smem, smem, vmem],
-        out_specs=(vmem, vmem, vmem),
+        in_specs=[hbm, vmem, hbm, vmem, vmem, smem, hbm],
+        out_specs=(hbm, vmem, vmem),
         scratch_shapes=[tiles(ROWT) for _ in range(8)] + [
+            tiles(slots), pltpu.VMEM((2048, 256), BF), pltpu.VMEM((2048, 256), BF),
+            ints(pltpu.VMEM, 2), ints(pltpu.SMEM, 2), ints(pltpu.VMEM, 1),
+            ints(pltpu.VMEM, 4), ints(pltpu.SMEM, 4),
             tiles(3, 8, 2), tiles(4, 8, 2), wide(8), wide(16),
             tiles(16), tiles(8, 2), tiles(16), tiles(16),
             pltpu.VMEM((128, 256), F32), pltpu.VMEM((NY, 16, 256), F32),
@@ -352,13 +391,14 @@
             tiles(3, 8, 2), tiles(4, 8, 2), wide(8), tiles(8, 16), tiles(8, 8),
             tiles(8, 8), tiles(8, 8), tiles(8, 8), tiles(3, 2), tiles(4, 2), wide(8),
             pltpu.SemaphoreType.DMA((COPIES,)), pltpu.SemaphoreType.DMA((COPIES,)),
-            pltpu.SemaphoreType.DMA((1,)),
+            pltpu.SemaphoreType.DMA((6,)),
         ],
         compiler_params=pltpu.CompilerParams(
             collective_id=1, has_side_effects=True, vmem_limit_bytes=56 << 20
         ),
         name="layer",
-    )(node_feats.reshape(ROWT, T, T), weight, tile_values, meta[:2], rq, cotangent)
+    )(node_feats.reshape(ROWT, T, T), weight, tile_values,
+      tile_cols.reshape(1, slots), tile_rows.reshape(1, slots), tile_count, cotangent)
     return outs
 
 

time: 129 us -> 118 us (0.915)
  starting transfers between devices: 5.89 us -> 0 us
  other arithmetic: 3.02 us -> 0 us
    ppermute x3 -> x0, starting transfers between devices: 5.89 us -> none  [body(): asked.append(lax.ppermute(row, 'blk', perm))]
  transfers between devices with their start and end apart: 3 -> 0, of which waited for: 1 -> 0; matrix products, arithmetic and copies ran while one was open for 0% -> 0% of each run, Pallas kernels for 0% -> 0%
where the time goes in v2:
time: 118 us; the launch traced here: 116 us
  Pallas kernels  112 us (95%)
  local copies, waits for them, and re-layouts  3.62 us (3%)
  between operations  1.3 us (1%)
    pallas_call x1, Pallas kernels, body(): pl.pallas_call(kernel, out_shape=(jax.ShapeDtypeStruct((2048, 256), BF),...  112 us
    unnamed x7, local copies, waits for them, and re-layouts  3.62 us

profile of v2, /device:TPU:1, one launch (start us, length us, event | category | flops | bytes accessed | tf_op | source)
XLA Modules:
  0.0 116.5 jit_solution(17581048295316755737)
XLA Ops:
  1.3 111.5 %layer.1 = (bf16[2048,256]{1,0:T(8,128)(2,1)}, f32[128,256]{1,0:T(8,128)}, f32[256,128]{1,0:T(8,128)}) custom-call(bf16[16,128,128]{2,1,0:T(8,128)(2,1)} %bitcast.3, bf16[128,256]{1,0:T(8,128)(2,1)} %weight.1, bf16[48,128,128]{2,1,0:T(8,128)(2,1)} %tile_values.1, s32[1,48]{1,0:T(1,128)} %bitcast.4, s32[1,48]{1,0:T(1,128)} %bitcast.5, s32[1]{0:T(128)S(6)} %copy.13.count, ...), custom_call_target="tpu_custom_call" | custom-call | tf_op jit(solution)/shard_map/layer/pallas_call | solution.py:374
  112.8 0.0 copy-start.1
  112.8 0.0 copy-start
  112.9 2.3 %copy.14 = bf16[2048,256]{1,0:T(8,128)(2,1)} copy(bf16[2048,256]{1,0:T(8,128)(2,1)} %get-tuple-element.6) | data formatting | bytes 2097152
  115.2 0.0 copy-done.1
  115.2 0.7 copy.15
  115.8 0.0 copy-done
  115.8 0.7 copy.16
Async XLA Ops:
  112.8 2.3 %copy-start.1 = (f32[128,256]{1,0:T(8,128)S(1)}, f32[128,256]{1,0:T(8,128)}, u32[]{:S(2)}) copy-start(f32[128,256]{1,0:T(8,128)} %get-tuple-element.7) | copy-start | bytes 393220
  112.8 3.0 %copy-start = (f32[256,128]{1,0:T(8,128)S(1)}, f32[256,128]{1,0:T(8,128)}, u32[]{:S(2)}) copy-start(f32[256,128]{1,0:T(8,128)} %get-tuple-element.8) | copy-start | bytes 393220

commit v3 on v2

--- a/solution.py
+++ b/solution.py
@@ -54,7 +54,7 @@
     layer_out, grad_weight, grad_feats,
     fb0, fb1, fb2, fb3, fb4, fb5, fb6, fb7,
     values, cot, lo, metav, meta, reqv, rqv, rq,
-    sy, got, prod, acc, sb, rb, agg, dagg, gwa, gwy, gwz, gwr,
+    sy, got, prod, acc, sb, rb, fxs, fxr, mine, agg, dagg, gwa, gwy, gwz, gwr,
     bs, br, unp, blkp, sr, zs, zp, zm, xs, xr, half,
     send_sem, recv_sem, local_sem,
 ):
@@ -191,46 +191,79 @@
     spmm(FWD[-2], False)
     spmm(FWD[-1], False)
 
-    def cast(t, carry):
-        sb[t] = acc[t].astype(BF)
-        return carry
-
-    lax.fori_loop(0, ROWT, cast, 0)
-    scattered = [
-        put(sb.at[pl.ds(2 * lax.rem(rep + d, REP), 2)], rb.at[REP - d], rpeer(d))
-        for d in range(1, REP)
-    ]
-    mine = acc[pl.ds(2 * rep, 2)]
-    for d, copy in enumerate(scattered, 1):
+    def home_tile(there, j):
+        return 4 * there + 2 * c + j
+
+    def other_tile(there, j):
+        return 4 * there + 2 * (1 - c) + j
+
+    order = [lax.rem(x + d, NX) for d in (2, 1, 3, 0)]
+    halves = []
+    for q, there in enumerate(order):
+        for j in range(2):
+            sb[q, j] = acc[other_tile(there, j)].astype(BF)
+        halves.append(put(sb.at[q], rb.at[q], sibling))
+    scattered = {}
+    for q, there in enumerate(order):
+        halves[q].wait_recv()
+        for j in range(2):
+            total = acc[home_tile(there, j)] + rb[q, j].astype(F32)
+            if q < 3:
+                fxs[q, j] = total.astype(BF)
+            else:
+                mine[j] = total
+        if q < 3:
+            d = (2, 1, 3)[q]
+            scattered[d] = put(fxs.at[q], fxr.at[NX - d], at(y, z, there, c))
+    for d in (1, 3, 2):
+        scattered[NX - d].wait_recv()
+        for j in range(2):
+            mine[j] += fxr[d, j].astype(F32)
+    own_pair = pl.ds(2 * rep, 2)
+    own_rows = pl.ds(pl.multiple_of(256 * rep, 256), 256)
+
+    def slope(a, cots):
+        pre = jnp.dot(a, weight[...], preferred_element_type=F32)
+        sig = jax.nn.sigmoid(pre)
+        dpre = (cots.astype(F32) * sig * (1.0 + pre * (1.0 - sig))).astype(BF)
+        return pre, sig, dpre
+
+    load_cot.wait()
+    agg[own_pair] = mine[...].astype(BF)
+    _, _, dpre_own = slope(mine[...].astype(BF).reshape(256, T), cot[own_rows, :])
+    back = lax.dot_general(dpre_own, weight[...], (((1,), (1,)), ((), ())), preferred_element_type=F32)
+    dagg[own_pair] = back.astype(BF).reshape(2, T, T)
+
+    def pair_of(xx, cc):
+        return pl.ds(2 * (2 * xx + cc), 2)
+
+    gathered = {d: put(dagg.at[own_pair], dagg.at[own_pair], at(y, z, lax.rem(x + d, NX), c)) for d in (2, 1, 3)}
+    passed = [put(dagg.at[own_pair], dagg.at[own_pair], sibling)]
+    for d in (1, 3, 2):
+        gathered[d].wait_recv()
+        piece = dagg.at[pair_of(lax.rem(x + NX - d, NX), c)]
+        passed.append(put(piece, piece, sibling))
+    for copy in passed:
         copy.wait_recv()
-        mine = mine + rb[REP - d].astype(F32)
-    agg[pl.ds(2 * rep, 2)] = mine.astype(BF)
-    pair = agg.at[pl.ds(2 * rep, 2)]
-    spread = [put(pair, pair, rpeer(d)) for d in range(1, REP)]
-    for copy in spread:
-        copy.wait_recv()
+    agg_all = [put(agg.at[own_pair], agg.at[own_pair], rpeer(d)) for d in range(1, REP)]
 
     gwa[...] = jnp.zeros_like(gwa)
-    load_cot.wait()
 
     def dense(i, carry):
         rows = pl.ds(pl.multiple_of(i * 256, 256), 256)
         a = agg[pl.ds(2 * i, 2)].reshape(256, T)
-        pre = jnp.dot(a, weight[...], preferred_element_type=F32)
-        sig = jax.nn.sigmoid(pre)
+        pre, sig, dpre = slope(a, cot[rows, :])
         lo[rows, :] = (pre * sig).astype(BF)
-        dpre = (cot[rows, :].astype(F32) * sig * (1.0 + pre * (1.0 - sig))).astype(BF)
         gwa[...] += lax.dot_general(a, dpre, (((0,), (0,)), ((), ())), preferred_element_type=F32)
-        back = lax.dot_general(dpre, weight[...], (((1,), (1,)), ((), ())), preferred_element_type=F32)
-        dagg[pl.ds(2 * i, 2)] = back.astype(BF).reshape(2, T, T)
         return carry
 
-    lax.fori_loop(0, 8, dense, 0)
-    store_lo.start()
-
     strip = pl.ds(pl.multiple_of(16 * rep, 16), 16)
-    gwy[pl.ds(y, 1)] = (gwa[strip, :] * (1.0 / 256.0))[None]
-    gw_y = [put(gwy.at[pl.ds(y, 1)], gwy.at[pl.ds(y, 1)], ypeer(d)) for d in range(1, NY)]
+    gw_y = []
+
+    def gw_first():
+        gwy[pl.ds(y, 1)] = (gwa[strip, :] * (1.0 / 256.0))[None]
+        for d in range(1, NY):
+            gw_y.append(put(gwy.at[pl.ds(y, 1)], gwy.at[pl.ds(y, 1)], ypeer(d)))
 
     back_sent = {}
 
@@ -340,9 +373,17 @@
             collect(BWD[i - 2])
         if 3 <= i:
             chain(BWD[i - 3])
-        if i == 4:
+        if i == 2:
+            for copy in agg_all:
+                copy.wait_recv()
+        if 2 <= i < 6:
+            lax.fori_loop(2 * i - 4, 2 * i - 2, dense, 0)
+        if i == 5:
+            store_lo.start()
+            gw_first()
+        if i == 7:
             gw_second()
-        if i == 7:
+        if i == 9:
             gw_third()
 
     x_sent = []
@@ -361,6 +402,20 @@
     store_lo.wait()
     for copy in used:
         copy.wait_send()
+
+
+def finish(lo, gw, gf, lo_out, gw_out, gf_out, lo_v, gw_v, gf_v, sems):
+    parts = [(lo.at[pl.ds(512 * i, 512)], lo_v.at[pl.ds(512 * i, 512)], lo_out.at[pl.ds(512 * i, 512)]) for i in range(4)]
+    parts += [(gw, gw_v, gw_out), (gf, gf_v, gf_out)]
+    loads = [pltpu.make_async_copy(a, v, sems.at[0, i]) for i, (a, v, _) in enumerate(parts)]
+    stores = [pltpu.make_async_copy(v, o, sems.at[1, i]) for i, (_, v, o) in enumerate(parts)]
+    for copy in loads:
+        copy.start()
+    for load, store in zip(loads, stores):
+        load.wait()
+        store.start()
+    for copy in stores:
+        copy.wait()
 
 
 def body(node_feats, weight, tile_values, tile_rows, tile_cols, tile_count, cotangent):
@@ -385,7 +440,7 @@
             ints(pltpu.VMEM, 2), ints(pltpu.SMEM, 2), ints(pltpu.VMEM, 1),
             ints(pltpu.VMEM, 4), ints(pltpu.SMEM, 4),
             tiles(3, 8, 2), tiles(4, 8, 2), wide(8), wide(16),
-            tiles(16), tiles(8, 2), tiles(16), tiles(16),
+            tiles(4, 2), tiles(4, 2), tiles(3, 2), tiles(4, 2), wide(2), tiles(16), tiles(16),
             pltpu.VMEM((128, 256), F32), pltpu.VMEM((NY, 16, 256), F32),
             pltpu.VMEM((NZ, 16, 256), F32), pltpu.VMEM((128, 256), F32),
             tiles(3, 8, 2), tiles(4, 8, 2), wide(8), tiles(8, 16), tiles(8, 8),
@@ -399,7 +454,14 @@
         name="layer",
     )(node_feats.reshape(ROWT, T, T), weight, tile_values,
       tile_cols.reshape(1, slots), tile_rows.reshape(1, slots), tile_count, cotangent)
-    return outs
+    return pl.pallas_call(
+        finish,
+        out_shape=tuple(jax.ShapeDtypeStruct(o.shape, o.dtype) for o in outs),
+        in_specs=[hbm] * 3,
+        out_specs=(hbm,) * 3,
+        scratch_shapes=[pltpu.VMEM(o.shape, o.dtype) for o in outs] + [pltpu.SemaphoreType.DMA((2, 6))],
+        name="finish",
+    )(*outs)
 
 
 def solution(mesh):

time: 118 us -> 112 us (0.949); the launches traced: 116 us -> 112 us
  local copies, waits for them, and re-layouts: 3.62 us -> 0 us
    unnamed x7 -> x0, local copies, waits for them, and re-layouts: 3.62 us -> none
    pallas_call x1, Pallas kernels: 112 us -> 109 us  [body(): pl.pallas_call(kernel, out_shape=(jax.ShapeDtypeStruct((2048, 256), BF),...]
    pallas_call x0 -> x1, Pallas kernels: none -> 2.1 us  [body(): pl.pallas_call(finish, out_shape=tuple((jax.ShapeDtypeStruct(o.shape, o.d...]
where the time goes in v3:
time: 112 us
  Pallas kernels  111 us (99%)
  between operations  1.29 us (1%)
    pallas_call x1, Pallas kernels, body(): pl.pallas_call(kernel, out_shape=(jax.ShapeDtypeStruct((2048, 256), BF),...  109 us

profile of v3, /device:TPU:1, one launch (start us, length us, event | category | flops | bytes accessed | tf_op | source)
XLA Modules:
  0.0 112.0 jit_solution(6302379692662796452)
XLA Ops:
  1.3 108.7 %layer.1 = (bf16[2048,256]{1,0:T(8,128)(2,1)}, f32[128,256]{1,0:T(8,128)}, f32[256,128]{1,0:T(8,128)}) custom-call(bf16[16,128,128]{2,1,0:T(8,128)(2,1)} %bitcast.3, bf16[128,256]{1,0:T(8,128)(2,1)} %weight.1, bf16[48,128,128]{2,1,0:T(8,128)(2,1)} %tile_values.1, s32[1,48]{1,0:T(1,128)} %bitcast.4, s32[1,48]{1,0:T(1,128)} %bitcast.5, s32[1]{0:T(128)S(6)} %copy.10.count, ...), custom_call_target="tpu_custom_call" | custom-call | tf_op jit(solution)/shard_map/layer/pallas_call | solution.py:429
  109.9 2.1 %finish.1 = (bf16[2048,256]{1,0:T(8,128)(2,1)}, f32[128,256]{1,0:T(8,128)}, f32[256,128]{1,0:T(8,128)}) custom-call(bf16[2048,256]{1,0:T(8,128)(2,1)} %get-tuple-element.6.lo, f32[128,256]{1,0:T(8,128)} %get-tuple-element.7.gw, f32[256,128]{1,0:T(8,128)} %get-tuple-element.8.gf), custom_call_target="tpu_custom_call" | custom-call | tf_op jit(solution)/shard_map/finish/pallas_call | solution.py:457

commit v4 on v3

--- a/solution.py
+++ b/solution.py
@@ -15,7 +15,7 @@
 REP = NX * NC
 ROWT = 16
 T = 128
-COPIES = 160
+COPIES = 176
 FWD = (0, 7, 1, 6, 2, 5, 3, 4)
 BWD = (4, 3, 5, 2, 6, 1, 7, 0)
 
@@ -55,7 +55,7 @@
     fb0, fb1, fb2, fb3, fb4, fb5, fb6, fb7,
     values, cot, lo, metav, meta, reqv, rqv, rq,
     sy, got, prod, acc, sb, rb, fxs, fxr, mine, agg, dagg, gwa, gwy, gwz, gwr,
-    bs, br, unp, blkp, sr, zs, zp, zm, xs, xr, half,
+    bs, br, unp, blkp, sr, zs, zp, zm, xs, xr, kept,
     send_sem, recv_sem, local_sem,
 ):
     blk = lax.axis_index("blk")
@@ -308,43 +308,46 @@
         lax.fori_loop(0, ROWT, add, 0)
         sib_sent[e] = put(blkp.at[e, pl.ds(8 * (1 - c), 8)], sr.at[e], sibling)
 
+    x_sent = {}
+
+    def across(e):
+        sib_sent[e].wait_recv()
+        for d in (2, 1, 3, 0):
+            there = lax.rem(x + d, NX)
+            for j in range(2):
+                total = blkp[e, 8 * c + 2 * there + j].astype(F32) + sr[e, 2 * there + j].astype(F32)
+                if d:
+                    xs[e, d - 1, j] = total.astype(BF)
+                else:
+                    kept[e, j] = total
+            if d:
+                x_sent[d, e] = put(xs.at[e, d - 1], xr.at[e, NX - d], at(y, z, there, c))
+
     zup, zdown = {}, {}
 
     def chain(e):
-        sib_sent[e].wait_recv()
-        if e == 0:
-            for j in range(2):
+        for d in range(1, NX):
+            x_sent[d, e].wait_recv()
+        for j in range(2):
+            total = kept[e, j]
+            for d in range(1, NX):
+                total = total + xr[e, d, j].astype(F32)
+            if e == 0:
                 zup[0, j].wait_recv()
                 zdown[0, j].wait_recv()
-
-            def home(t, carry):
-                half[t] = (
-                    blkp[0, 8 * c + t].astype(F32) + sr[0, t].astype(F32)
-                    + zp[0, t].astype(F32) + zm[0, t].astype(F32)
-                )
-                return carry
-
-            lax.fori_loop(0, 8, home, 0)
-            return
-        for j in range(2):
+                total = total + zp[0, j].astype(F32) + zm[0, j].astype(F32)
+                grad_feats[pl.ds(T * j, T), :] = total
+                continue
             rising = e < 4 or (e == 4 and j == 0)
             begins = e == 4 or (e == 3 and j == 1) or (e == 5 and j == 0)
             if not begins:
                 (zup if rising else zdown)[e, j].wait_recv()
-
-            def step(t, carry):
-                total = blkp[e, 8 * c + t].astype(F32) + sr[e, t].astype(F32)
-                if not begins:
-                    total = total + (zp if rising else zm)[e % 8, t].astype(F32)
-                zs[e, t] = total.astype(BF)
-                return carry
-
-            lax.fori_loop(4 * j, 4 * j + 4, step, 0)
-            piece = pl.ds(4 * j, 4)
+                total = total + (zp if rising else zm)[e, j].astype(F32)
+            zs[e, j] = total.astype(BF)
             if rising:
-                zup[e - 1, j] = put(zs.at[e, piece], zp.at[e - 1, piece], zpeer(1))
+                zup[e - 1, j] = put(zs.at[e, j], zp.at[e - 1, j], zpeer(1))
             else:
-                zdown[(e + 1) % 8, j] = put(zs.at[e, piece], zm.at[(e + 1) % 8, piece], zpeer(NZ - 1))
+                zdown[(e + 1) % 8, j] = put(zs.at[e, j], zm.at[(e + 1) % 8, j], zpeer(NZ - 1))
 
     gw_z, gw_r = [], []
 
@@ -365,40 +368,34 @@
         for d in range(1, REP):
             gw_r.append(put(gwr.at[strip], gwr.at[strip], rpeer(d)))
 
+    lead = 3
+    for i in range(lead):
+        products(BWD[i])
     n = len(BWD)
-    for i in range(n + 3):
-        if i < n:
-            products(BWD[i])
-        if 2 <= i < n + 2:
-            collect(BWD[i - 2])
-        if 3 <= i:
-            chain(BWD[i - 3])
-        if i == 2:
+    for i in range(n):
+        collect(BWD[i])
+        if i + lead < n:
+            products(BWD[i + lead])
+        if i == 0:
             for copy in agg_all:
                 copy.wait_recv()
-        if 2 <= i < 6:
-            lax.fori_loop(2 * i - 4, 2 * i - 2, dense, 0)
-        if i == 5:
+        if i < 4:
+            lax.fori_loop(2 * i, 2 * i + 2, dense, 0)
+        across(BWD[i])
+        if i:
+            chain(BWD[i - 1])
+        if i == 3:
             store_lo.start()
             gw_first()
-        if i == 7:
+        if i == 4:
             gw_second()
-        if i == 9:
+        if i == 6:
             gw_third()
-
-    x_sent = []
-    for d in range(1, NX):
-        there = lax.rem(x + d, NX)
-        xs[d - 1] = half[pl.ds(2 * there, 2)].astype(BF)
-        x_sent.append(put(xs.at[d - 1], xr.at[NX - d], at(y, z, there, c)))
-    total = half[pl.ds(2 * x, 2)]
+    chain(BWD[-1])
+
     for copy in gw_r:
         copy.wait_recv()
     grad_weight[...] = gwr[...]
-    for d, copy in enumerate(x_sent, 1):
-        copy.wait_recv()
-        total = total + xr[NX - d].astype(F32)
-    grad_feats[...] = total.reshape(2 * T, T)
     store_lo.wait()
     for copy in used:
         copy.wait_send()
@@ -444,7 +441,7 @@
             pltpu.VMEM((128, 256), F32), pltpu.VMEM((NY, 16, 256), F32),
             pltpu.VMEM((NZ, 16, 256), F32), pltpu.VMEM((128, 256), F32),
             tiles(3, 8, 2), tiles(4, 8, 2), wide(8), tiles(8, 16), tiles(8, 8),
-            tiles(8, 8), tiles(8, 8), tiles(8, 8), tiles(3, 2), tiles(4, 2), wide(8),
+            tiles(8, 2), tiles(8, 2), tiles(8, 2), tiles(8, 3, 2), tiles(8, 4, 2), wide(8, 2),
             pltpu.SemaphoreType.DMA((COPIES,)), pltpu.SemaphoreType.DMA((COPIES,)),
             pltpu.SemaphoreType.DMA((6,)),
         ],

time: 112 us -> 108 us (0.964)
  Pallas kernels: 111 us -> 107 us
    pallas_call x1, Pallas kernels: 109 us -> 105 us  [body(): pl.pallas_call(kernel, out_shape=(jax.ShapeDtypeStruct((2048, 256), BF),...]
where the time goes in v4:
time: 108 us
  Pallas kernels  107 us (99%)
  between operations  1.29 us (1%)
    pallas_call x1, Pallas kernels, body(): pl.pallas_call(kernel, out_shape=(jax.ShapeDtypeStruct((2048, 256), BF),...  105 us

profile of v4, /device:TPU:1, one launch (start us, length us, event | category | flops | bytes accessed | tf_op | source)
XLA Modules:
  0.0 108.2 jit_solution(17451996501120841264)
XLA Ops:
  1.3 104.8 %layer.1 = (bf16[2048,256]{1,0:T(8,128)(2,1)}, f32[128,256]{1,0:T(8,128)}, f32[256,128]{1,0:T(8,128)}) custom-call(bf16[16,128,128]{2,1,0:T(8,128)(2,1)} %bitcast.3, bf16[128,256]{1,0:T(8,128)(2,1)} %weight.1, bf16[48,128,128]{2,1,0:T(8,128)(2,1)} %tile_values.1, s32[1,48]{1,0:T(1,128)} %bitcast.4, s32[1,48]{1,0:T(1,128)} %bitcast.5, s32[1]{0:T(128)S(6)} %copy.10.count, ...), custom_call_target="tpu_custom_call" | custom-call | tf_op jit(solution)/shard_map/layer/pallas_call | solution.py:426
  106.1 2.1 %finish.1 = (bf16[2048,256]{1,0:T(8,128)(2,1)}, f32[128,256]{1,0:T(8,128)}, f32[256,128]{1,0:T(8,128)}) custom-call(bf16[2048,256]{1,0:T(8,128)(2,1)} %get-tuple-element.6.lo, f32[128,256]{1,0:T(8,128)} %get-tuple-element.7.gw, f32[256,128]{1,0:T(8,128)} %get-tuple-element.8.gf), custom_call_target="tpu_custom_call" | custom-call | tf_op jit(solution)/shard_map/finish/pallas_call | solution.py:454

commit v5 on v4

--- a/solution.py
+++ b/solution.py
@@ -16,7 +16,6 @@
 ROWT = 16
 T = 128
 COPIES = 176
-FWD = (0, 7, 1, 6, 2, 5, 3, 4)
 BWD = (4, 3, 5, 2, 6, 1, 7, 0)
 
 
@@ -173,23 +172,29 @@
 
         lax.fori_loop(0, ROWT, add, 0)
 
-    for i, e in enumerate(FWD):
-        if e:
-            arrive(e)
-            if i >= 2:
-                spmm(FWD[i - 2], i == 2)
-            for j in range(2):
-                shared[e, j].wait_recv()
-        else:
-            for copy in asked:
-                copy.wait_recv()
-            load_rq.start()
-            load_meta.wait()
-            load_values.wait()
-            load_rq.wait()
+    def finish_block(e):
+        for j in range(2):
+            shared[e, j].wait_recv()
         pack(e)
-    spmm(FWD[-2], False)
-    spmm(FWD[-1], False)
+
+    for copy in asked:
+        copy.wait_recv()
+    load_rq.start()
+    load_meta.wait()
+    load_values.wait()
+    load_rq.wait()
+    pack(0)
+    for near, far, ready in ((7, 1, ()), (6, 2, (0,)), (5, 3, (7,))):
+        arrive(near)
+        arrive(far)
+        finish_block(near)
+        finish_block(far)
+        for e in ready:
+            spmm(e, e == 0)
+    arrive(4)
+    finish_block(4)
+    for e in (1, 6, 2, 5, 3, 4):
+        spmm(e, False)
 
     def home_tile(there, j):
         return 4 * there + 2 * c + j

time: 108 us -> 105 us (0.972)
  Pallas kernels: 107 us -> 104 us
    pallas_call x1, Pallas kernels: 105 us -> 102 us  [body(): pl.pallas_call(kernel, out_shape=(jax.ShapeDtypeStruct((2048, 256), BF),...]
where the time goes in v5:
time: 105 us
  Pallas kernels  104 us (99%)
  between operations  1.29 us (1%)
    pallas_call x1, Pallas kernels, body(): pl.pallas_call(kernel, out_shape=(jax.ShapeDtypeStruct((2048, 256), BF),...  102 us

profile of v5, /device:TPU:1, one launch (start us, length us, event | category | flops | bytes accessed | tf_op | source)
XLA Modules:
  0.0 105.0 jit_solution(16281143015797154831)
XLA Ops:
  1.3 101.6 %layer.1 = (bf16[2048,256]{1,0:T(8,128)(2,1)}, f32[128,256]{1,0:T(8,128)}, f32[256,128]{1,0:T(8,128)}) custom-call(bf16[16,128,128]{2,1,0:T(8,128)(2,1)} %bitcast.3, bf16[128,256]{1,0:T(8,128)(2,1)} %weight.1, bf16[48,128,128]{2,1,0:T(8,128)(2,1)} %tile_values.1, s32[1,48]{1,0:T(1,128)} %bitcast.4, s32[1,48]{1,0:T(1,128)} %bitcast.5, s32[1]{0:T(128)S(6)} %copy.10.count, ...), custom_call_target="tpu_custom_call" | custom-call | tf_op jit(solution)/shard_map/layer/pallas_call | solution.py:431
  102.9 2.1 %finish.1 = (bf16[2048,256]{1,0:T(8,128)(2,1)}, f32[128,256]{1,0:T(8,128)}, f32[256,128]{1,0:T(8,128)}) custom-call(bf16[2048,256]{1,0:T(8,128)(2,1)} %get-tuple-element.6.lo, f32[128,256]{1,0:T(8,128)} %get-tuple-element.7.gw, f32[256,128]{1,0:T(8,128)} %get-tuple-element.8.gf), custom_call_target="tpu_custom_call" | custom-call | tf_op jit(solution)/shard_map/finish/pallas_call | solution.py:459
